TPU v7x, 512 devices: a whole 4x4x16 slice. The times are simulated.
512 devices in a mesh: row: 64 (over x, z_lo, core), col: 8 (over y, z_hi).
Axes of the slice: x: 4, y: 4, z: 16 (z_hi: 2, z_lo: 8; z = z_hi * 8 + z_lo), core: 2. Of those that a mesh axis runs over, the one named last changes fastest.
Arguments:
- object_slices: float32 [2, 2, 8192, 1024], P(None, None, 'row', 'col'), may hold values from -4 to 4
- probe_field: float32 [2, 128, 128], replicated, may hold values from -6 to 6
- measured: float32 [2048, 128, 128], P(('row', 'col')), may hold values from 0.5 to 4
- offsets: int32 [2048, 2], P(('row', 'col')), may hold values from 0 to 127
- counts: int32 [512], P(('row', 'col')), may hold values from 1 to 4, 1024 in all
Outputs:
- object_grad: float32 [2, 2, 8192, 1024], P(None, None, 'row', 'col')
- probe_grad: float32 [2, 128, 128], replicated
Inputs may be any that keep to these rules, and one draw needn't show every extreme that they name: `counts`: live slots of each owner tile; they sum to 1024 and some tile has exactly 4.
All inputs are finite; a program needn't handle non-finite values. No bound on the sum of `counts` on one device may be relied on, other than what follows from the above.
Results may differ from a plain program's by a relative error of at most 0.0003.
Values sent between devices are 32-bit elements; how exact they have to be, the bound alone decides.
A program may use at most 64 MiB of HBM per device.

v0:
```python
import math

import jax
import jax.numpy as jnp
from jax import lax
from jax.sharding import PartitionSpec as P

PROP = 40.0


def from_behind(x, axis, by):
    peers = lax.axis_size(axis)
    return lax.ppermute(x, axis, [(i, (i + by) % peers) for i in range(peers)])


def matmul_high(left, right):
    return jnp.matmul(left, right, precision=lax.Precision.HIGHEST)


def dft_tables(extent):
    counter = jnp.arange(extent, dtype=jnp.int32)
    products = counter[:, None] * counter[None, :] % extent
    phases = -2.0 * math.pi / extent * products.astype(jnp.float32)
    factor = 1.0 / math.sqrt(extent)
    return (jnp.cos(phases) * factor, jnp.sin(phases) * factor)


def propagator(extent):
    counter = jnp.arange(extent, dtype=jnp.int32)
    freq = jnp.where(counter < extent // 2, counter, counter - extent).astype(jnp.float32)
    phases = PROP * (freq[:, None] ** 2 + freq[None, :] ** 2) / (extent * extent)
    return (jnp.cos(phases), -jnp.sin(phases))


def transform(real_part, imag_part, table_real, table_imag):
    left_real = matmul_high(table_real, real_part) - matmul_high(table_imag, imag_part)
    left_imag = matmul_high(table_real, imag_part) + matmul_high(table_imag, real_part)
    out_real = matmul_high(left_real, table_real) - matmul_high(left_imag, table_imag)
    out_imag = matmul_high(left_real, table_imag) + matmul_high(left_imag, table_real)
    return (out_real, out_imag)


def slot_losses(patches, probe_now, target, tables):
    table_real, table_imag, kernel_real, kernel_imag = tables
    wave_real, wave_imag = (probe_now[0], probe_now[1])
    layers = patches.shape[-4]
    for slice_index in range(layers):
        obj_real = patches[..., slice_index, 0, :, :]
        obj_imag = patches[..., slice_index, 1, :, :]
        wave_real, wave_imag = (
            wave_real * obj_real - wave_imag * obj_imag,
            wave_real * obj_imag + wave_imag * obj_real,
        )
        if slice_index < layers - 1:
            spec_real, spec_imag = transform(wave_real, wave_imag, table_real, table_imag)
            spec_real, spec_imag = (
                spec_real * kernel_real - spec_imag * kernel_imag,
                spec_real * kernel_imag + spec_imag * kernel_real,
            )
            wave_real, wave_imag = transform(spec_real, spec_imag, table_real, -table_imag)
    far_real, far_imag = transform(wave_real, wave_imag, table_real, table_imag)
    excess = far_real * far_real + far_imag * far_imag - target
    return 0.5 * jnp.sum(excess * excess, axis=(-2, -1))


def per_device(object_slices, probe_field, measured, offsets, counts):
    extent = probe_field.shape[-1]
    layers = object_slices.shape[0]
    tile_rows = object_slices.shape[2]
    tile_cols = object_slices.shape[3]
    slots = offsets.shape[0]
    below = from_behind(object_slices, "row", -1)
    taller = jnp.concatenate([object_slices, below], axis=2)
    beside = from_behind(taller, "col", -1)
    extended = jnp.concatenate([taller, beside], axis=3)
    table_real, table_imag = dft_tables(extent)
    kernel_real, kernel_imag = propagator(extent)
    tables = (table_real, table_imag, kernel_real, kernel_imag)
    live_count = counts[0]
    live_mask = (jnp.arange(slots, dtype=jnp.int32) < live_count).astype(jnp.float32)

    def masked_loss(field, probe_now):
        patches = jax.vmap(
            lambda corner: lax.dynamic_slice(
                field, (0, 0, corner[0], corner[1]), (layers, 2, extent, extent)
            )
        )(offsets)
        return jnp.sum(live_mask * slot_losses(patches, probe_now, measured, tables))

    loss_value, pullback = jax.vjp(masked_loss, extended, probe_field)
    grad_extended, grad_probe = pullback(jnp.ones((), jnp.float32))
    right_rim = grad_extended[:, :, :, tile_cols:]
    from_left = from_behind(right_rim, "col", 1)
    narrow = grad_extended[:, :, :, :tile_cols].at[:, :, :, :extent].add(from_left)
    lower_rim = narrow[:, :, tile_rows:, :]
    from_above = from_behind(lower_rim, "row", 1)
    object_grad = narrow[:, :, :tile_rows, :].at[:, :, :extent, :].add(from_above)
    summed = lax.psum(grad_probe, ("row", "col"))
    positions = lax.axis_size("row") * lax.axis_size("col") * slots
    return (object_grad, summed * (1.0 / math.sqrt(positions)))


def solution(mesh):
    in_specs = (
        P(None, None, "row", "col"),
        P(),
        P(("row", "col"), None, None),
        P(("row", "col"), None),
        P(("row", "col")),
    )
    out_specs = (P(None, None, "row", "col"), P())
    return jax.shard_map(
        per_device, mesh=mesh, in_specs=in_specs, out_specs=out_specs, check_vma=False
    )
```

profile of v0, /device:TPU:1, one launch (start us, length us, event | category | flops | bytes accessed | tf_op | source)
XLA Modules:
  0.0 634.0 jit_solution(15122743623015499740)
XLA Ops:
  7.2 8.8 %collective-permute-start = (f32[2,2,128,128]{3,2,1,0:T(8,128)}, f32[2,2,128,128]{3,2,1,0:T(8,128)S(1)}, u32[]{:S(2)}, u32[]{:S(2)}) collective-permute-start(f32[2,2,128,128]{3,2,1,0:T(8,128)} %param.13), channel_id=1, source_target_pairs={{0,504},{8,0},{16,8},{24,16},{32,24},{40,32},{48,40},{56,48},{64,5... | collective-permute-start | bytes 786440 | tf_op jit(solution)/shard_map/ppermute | solution.py:13
  16.0 1.0 constant_dynamic-update-slice_fusion.1
  18.7 15.4 %collective-permute-start.1 = (f32[2,2,256,128]{3,2,1,0:T(8,128)S(1)}, f32[2,2,256,128]{3,2,1,0:T(8,128)S(1)}, u32[]{:S(2)}, u32[]{:S(2)}) collective-permute-start(f32[2,2,256,128]{3,2,1,0:T(8,128)S(1)} %constant_dynamic-update-slice_fusion), channel_id=1, source_target_pairs={{0,7},{1,0},{2,1},{3,2},{4,3},{5,4},{6,5},{7,6},{8,15},{9,8},{10,9... | collective-permute-start | bytes 1572872 | tf_op jit(solution)/shard_map/ppermute | solution.py:13
  34.4 12.8 %collective-permute-done.1 = f32[2,2,256,128]{3,2,1,0:T(8,128)S(1)} collective-permute-done((f32[2,2,256,128]{3,2,1,0:T(8,128)S(1)}, f32[2,2,256,128]{3,2,1,0:T(8,128)S(1)}, u32[]{:S(2)}, u32[]{:S(2)}) %collective-permute-start.1) | collective-permute-done | bytes 524320 | tf_op jit(solution)/shard_map/ppermute | solution.py:13
  47.3 8.4 %while.6 = (s32[]{:T(128)}, f32[2,2,256,256]{3,2,1,0:T(8,128)S(1)}, s32[4,4]{1,0:T(4,128)S(1)}, f32[4,2,2,128,128]{4,3,0,2,1:T(8,128)S(1)}, s32[]{:T(128)}) while((s32[]{:T(128)}, f32[2,2,256,256]{3,2,1,0:T(8,128)S(1)}, s32[4,4]{1,0:T(4,128)S(1)}, f32[4,2,2,128,128]{4,3,0,2,1:T(8,128)S(1)}, s32[]{:T(128)}) %tuple.73), condition=%wide.while_cond.2, body=%wide.while_body.2.sunk | while | flops 2 | bytes 524413 | solution.py:84
  47.3 0.7 fusion.411
  48.0 1.4 bitcast_dynamic-update-slice_fusion.2
  49.4 0.7 fusion.411
  50.1 1.4 bitcast_dynamic-update-slice_fusion.2
  51.5 0.7 fusion.411
  52.1 1.4 bitcast_dynamic-update-slice_fusion.2
  53.6 0.7 fusion.411
  54.2 1.4 bitcast_dynamic-update-slice_fusion.2
  55.6 0.7 fusion.103
  56.3 0.7 fusion.107
  57.0 0.7 fusion.17
  58.9 0.7 fusion.16
  60.9 0.7 fusion.96
  61.6 0.7 fusion.100
  62.3 0.7 fusion.15
  64.2 0.7 fusion.14
  65.5 0.7 fusion.19
  66.2 0.7 fusion.91
  66.8 0.7 fusion.93
  68.8 0.8 fusion.88
  69.6 0.6 fusion.12
  71.2 0.7 add_multiply_fusion
  73.8 0.7 fusion.54
  74.4 0.6 fusion.84
  75.7 0.7 fusion.8
  76.4 0.8 add_bitcast_fusion.3
  79.0 0.6 fusion.78
  79.7 0.7 fusion.37
  81.0 0.7 fusion.5
  81.7 0.7 fusion.4
  82.3 0.8 fusion.51
  84.4 0.7 fusion.48
  85.1 0.6 fusion.72
  86.4 0.7 fusion
  87.0 0.8 fusion.24
  88.0 42.1 %while.7 = (s32[]{:T(128)}, f32[2,2,256,256]{3,2,1,0:T(8,128)S(1)}, s32[4,4]{1,0:T(4,128)S(1)}, f32[4,2,2,128,128]{4,3,0,2,1:T(8,128)S(1)}, s32[]{:T(128)}, /*index=5*/s32[4]{0:T(128)S(1)}, s32[]{:T(128)}) while((s32[]{:T(128)}, f32[2,2,256,256]{3,2,1,0:T(8,128)S(1)}, s32[4,4]{1,0:T(4,128)S(1)}, f32[4,2,2,128,128]{4,3,0,2,1:T(8,128)S(1)}, ...), condition=%wide.while_cond.3, body=%wide.while_body.3.sunk | while | flops 131101 | bytes 1310915 | solution.py:84
  88.0 0.7 fusion.412
  88.7 3.3 and_reduce_fusion.2
  92.0 2.0 add_select_fusion.3
  94.0 4.5 dynamic-update-slice.16
  98.6 0.7 fusion.412
  99.3 3.3 and_reduce_fusion.2
  102.6 2.0 add_select_fusion.3
  104.6 4.4 dynamic-update-slice.16
  109.0 0.7 fusion.412
  109.7 3.3 and_reduce_fusion.2
  113.0 2.0 add_select_fusion.3
  115.0 4.3 dynamic-update-slice.16
  119.4 0.7 fusion.412
  120.1 3.3 and_reduce_fusion.2
  123.4 2.0 add_select_fusion.3
  125.4 4.6 dynamic-update-slice.16
  130.1 4.6 collective-permute-start.2
  134.7 0.7 pad_add_fusion.1
  135.4 16.4 %collective-permute-done.2 = f32[2,2,256,128]{3,2,1,0:T(8,128)S(1)} collective-permute-done((f32[2,2,256,128]{3,2,1,0:T(8,128)S(1)}, f32[2,2,256,128]{3,2,1,0:T(8,128)S(1)}, u32[]{:S(2)}, u32[]{:S(2)}) %collective-permute-start.2) | collective-permute-done | bytes 524320 | tf_op jit(solution)/shard_map/ppermute | solution.py:13
  151.9 60.7 %collective-permute-start.3 = (f32[2,2,128,128]{3,2,1,0:T(8,128)S(1)}, f32[2,2,128,128]{3,2,1,0:T(8,128)S(1)}, u32[]{:S(2)}, u32[]{:S(2)}) collective-permute-start(f32[2,2,128,128]{3,2,1,0:T(8,128)S(1)} %slice.139), channel_id=1, source_target_pairs={{0,8},{8,16},{16,24},{24,32},{32,40},{40,48},{48,56},{56,64},{64,7... | collective-permute-start | bytes 786440 | tf_op jit(solution)/shard_map/ppermute | solution.py:13
  212.6 412.3 %all-reduce.8.cloned.1.call-done = f32[2,128,128]{2,1,0:T(8,128)} async-done(((f32[2,128,128]{2,1,0:T(8,128)}), f32[2,128,128]{2,1,0:T(8,128)}) %all-reduce.8.cloned.1.call-update) | async-done | bytes 131088 | tf_op jit(solution)/shard_map/psum | solution.py:98
  624.9 1.6 broadcast_multiply_fusion
  626.5 0.7 slice_add_fusion.1
  (62 shorter events, 15.1 us)
Async XLA Ops:
  7.2 9.8 %copy-start.3 = (s32[4,2]{0,1:T(2,128)S(1)}, s32[4,2]{0,1:T(2,128)}, u32[]{:S(2)}) copy-start(s32[4,2]{0,1:T(2,128)} %param.16) | copy-start | bytes 100
  7.2 617.7 %all-reduce.8.cloned.1.call-start = ((), (), s32[]{:S(2)}) async-start(), calls=%async_computation | async-start | bytes 262144 | tf_op jit(solution)/shard_map/psum | solution.py:98
  7.2 11.4 %collective-permute-start = (f32[2,2,128,128]{3,2,1,0:T(8,128)}, f32[2,2,128,128]{3,2,1,0:T(8,128)S(1)}, u32[]{:S(2)}, u32[]{:S(2)}) collective-permute-start(f32[2,2,128,128]{3,2,1,0:T(8,128)} %param.13), channel_id=1, source_target_pairs={{0,504},{8,0},{16,8},{24,16},{32,24},{40,32},{48,40},{56,48},{64,5... | collective-permute-start | bytes 786440 | tf_op jit(solution)/shard_map/ppermute | solution.py:13
  17.9 0.7 copy-start.2
  18.6 15.7 %copy-start.1 = (f32[2,128,128]{2,1,0:T(8,128)S(1)}, f32[2,128,128]{2,1,0:T(8,128)}, u32[]{:S(2)}) copy-start(f32[2,128,128]{2,1,0:T(8,128)} %param.14) | copy-start | bytes 393220
  18.7 28.6 %collective-permute-start.1 = (f32[2,2,256,128]{3,2,1,0:T(8,128)S(1)}, f32[2,2,256,128]{3,2,1,0:T(8,128)S(1)}, u32[]{:S(2)}, u32[]{:S(2)}) collective-permute-start(f32[2,2,256,128]{3,2,1,0:T(8,128)S(1)} %constant_dynamic-update-slice_fusion), channel_id=1, source_target_pairs={{0,7},{1,0},{2,1},{3,2},{4,3},{5,4},{6,5},{7,6},{8,15},{9,8},{10,9... | collective-permute-start | bytes 1572872 | tf_op jit(solution)/shard_map/ppermute | solution.py:13
  70.2 1.0 copy-start
  130.1 21.7 %collective-permute-start.2 = (f32[2,2,256,128]{3,2,1,0:T(8,128)S(1)}, f32[2,2,256,128]{3,2,1,0:T(8,128)S(1)}, u32[]{:S(2)}, u32[]{:S(2)}) collective-permute-start(f32[2,2,256,128]{3,2,1,0:T(8,128)S(1)} %slice.93), channel_id=1, source_target_pairs={{0,1},{1,2},{2,3},{3,4},{4,5},{5,6},{6,7},{7,0},{8,9},{9,10},{10,1... | collective-permute-start | bytes 1572872 | tf_op jit(solution)/shard_map/ppermute | solution.py:13
  151.9 474.5 %collective-permute-start.3 = (f32[2,2,128,128]{3,2,1,0:T(8,128)S(1)}, f32[2,2,128,128]{3,2,1,0:T(8,128)S(1)}, u32[]{:S(2)}, u32[]{:S(2)}) collective-permute-start(f32[2,2,128,128]{3,2,1,0:T(8,128)S(1)} %slice.139), channel_id=1, source_target_pairs={{0,8},{8,16},{16,24},{24,32},{32,40},{40,48},{48,56},{56,64},{64,7... | collective-permute-start | bytes 786440 | tf_op jit(solution)/shard_map/ppermute | solution.py:13
Sparse Core Ops, SparseCore 0:
  135.5 489.3 all-reduce.7
where the time goes:
time: 634 us
  waiting for transfers between devices  442 us (70%)
  starting transfers between devices  89.4 us (14%)
  matrix products  31.5 us (5%)
  local copies, waits for them, and re-layouts  31.1 us (5%)
  other arithmetic  25 us (4%)
  between operations  15.3 us (2%)
    psum x1, waiting for transfers between devices, per_device(): summed = lax.psum(grad_probe, ('row', 'col'))  412 us
    ppermute x4, starting transfers between devices, from_behind(): return lax.ppermute(x, axis, [(i, (i + by) % peers) for i in range(peers)])  89.4 us
    dot_general x48, matrix products, matmul_high(): return jnp.matmul(left, right, precision=lax.Precision.HIGHEST)  31.5 us
    ppermute x4, waiting for transfers between devices, from_behind(): return lax.ppermute(x, axis, [(i, (i + by) % peers) for i in range(peers)])  29.3 us
    scatter-add x8, other arithmetic  21.4 us
    scatter-add x12, local copies, waits for them, and re-layouts  20.6 us
  transfers between devices with their start and end apart: 5, of which 3 were waited for; matrix products, arithmetic and copies ran while one was open for 1% of the time, Pallas kernels for 0%

commit v1 on v0

v1 whole, which is shorter than its diff:
```python
import functools
import math

import jax
import jax.numpy as jnp
import ml_dtypes
import numpy as np
from jax import lax
from jax.experimental import pallas as pl
from jax.experimental.pallas import tpu as pltpu
from jax.sharding import PartitionSpec as P

PROP = 40.0
W = 128
CAP = 4
MESH = pl.DeviceIdType.MESH
F32 = jnp.float32
BF16 = jnp.bfloat16


def _tables():
    k = np.arange(W)
    dft = np.exp(-2j * np.pi * (np.outer(k, k) % W) / W) / math.sqrt(W)
    freq = np.where(k < W // 2, k, k - W).astype(np.float64)
    h = np.exp(-1j * PROP * freq**2 / (W * W))
    prop = np.conj(dft) @ (h[:, None] * dft)
    out = np.zeros((2, 6, W, W), ml_dtypes.bfloat16)
    for t, table in enumerate((prop, dft)):
        for j, part in enumerate((table.real, table.imag, -table.imag)):
            part = part.astype(np.float32)
            high = part.astype(ml_dtypes.bfloat16)
            out[t, j] = high
            out[t, 3 + j] = (part - high.astype(np.float32)).astype(ml_dtypes.bfloat16)
    return out


def _split(x):
    high = x.astype(BF16)
    return high, (x - high.astype(F32)).astype(BF16)


def _blocks(tab, conj):
    parts = []
    for base in (0, 3):
        re, im, neg = tab[base], tab[base + 1], tab[base + 2]
        if conj:
            im, neg = neg, im
        parts.append(jnp.concatenate([jnp.concatenate([re, im], 1), jnp.concatenate([neg, re], 1)], 0))
    return parts


def _two_sided(fields, tab, conj):
    n = len(fields)
    wh, wl = _blocks(tab, conj)
    vh, vl = _blocks(tab, not conj)
    stacked = jnp.concatenate([jnp.concatenate([re, im], 1) for re, im in fields], 0)
    high, low = _split(stacked)
    y = jnp.dot(
        jnp.concatenate([high, low, high], 1), jnp.concatenate([wh, wh, wl], 0), preferred_element_type=F32
    )
    beside = jnp.concatenate(
        [jnp.concatenate([y[s * W : (s + 1) * W, :W], y[s * W : (s + 1) * W, W:]], 0) for s in range(n)], 1
    )
    high, low = _split(beside)
    z = jnp.dot(
        jnp.concatenate([vh, vh, vl], 1), jnp.concatenate([high, low, high], 0), preferred_element_type=F32
    )
    return [(z[:W, s * W : (s + 1) * W], z[W:, s * W : (s + 1) * W]) for s in range(n)]


def _mul(a, b):
    return a[0] * b[0] - a[1] * b[1], a[0] * b[1] + a[1] * b[0]


def _mul_conj(a, b):
    return a[0] * b[0] + a[1] * b[1], a[1] * b[0] - a[0] * b[1]


def _xor(i, k):
    if k == 0:
        return i
    if k == 1:
        return i + 1 - 2 * lax.rem(i, 2)
    if k == 2:
        return lax.rem(i + 2, 4)
    return 3 - i


def _kernel(
    n_row, n_col, offs, cnt, obj, probe_hbm, meas_hbm, tab_hbm, out, pout,
    own, right, below, diag, g_own, g_right, g_below, g_diag, r_right, r_below, r_diag,
    probe, meas, tab, gp, core_in, xy_in, za_in, zb_in, plane,
    local, fc_s, fc_r, fr_s, fr_r, fd_s, fd_r, bb_s, bb_r, bd_s, bd_r, bc_s, bc_r,
    core_s, core_r, xy_s, xy_r, za_s, za_r, zb_s, zb_r, ag_s, ag_r, cg_s, cg_r,
):
    row, col = lax.axis_index("row"), lax.axis_index("col")
    core = lax.rem(row, 2)
    z_lo = lax.rem(row // 2, 8)
    x = row // 16
    z_hi = lax.rem(col, 2)
    y = col // 2

    def at(x_, y_, zl, zh, core_):
        return ((x_ * 8 + zl) * 2 + core_, y_ * 2 + zh)

    up = (lax.rem(row + n_row - 1, n_row), col)
    down = (lax.rem(row + 1, n_row), col)
    lft = (row, lax.rem(col + n_col - 1, n_col))
    rgt = (row, lax.rem(col + 1, n_col))
    partner = at(x, y, z_lo, z_hi, 1 - core)
    xy_peers = [
        (_xor(x, k // 4), _xor(y, k % 4)) for k in range(16)
    ]
    za_peers = [at(x, y, (z_lo // 4) * 4 + _xor(lax.rem(z_lo, 4), k), z_hi, core) for k in range(4)]
    zb_peers = [
        at(x, y, lax.rem(z_lo + 4 * (k % 2), 8), z_hi if k < 2 else 1 - z_hi, core) for k in range(4)
    ]
    peers = [up, down, lft, rgt, partner]
    peers += [at(px, py, z_lo, z_hi, core) for px, py in xy_peers[1:]]
    peers += za_peers[1:] + zb_peers[1:]
    barrier = pltpu.get_barrier_semaphore()
    for peer in peers:
        pl.semaphore_signal(barrier, inc=1, device_id=peer, device_id_type=MESH)

    loads = [
        pltpu.make_async_copy(obj, own, local.at[0]),
        pltpu.make_async_copy(probe_hbm, probe, local.at[1]),
        pltpu.make_async_copy(meas_hbm, meas, local.at[2]),
        pltpu.make_async_copy(tab_hbm, tab, local.at[3]),
    ]
    for load in loads:
        load.start()

    def send(src, dst, s, r, to):
        copy = pltpu.make_async_remote_copy(
            src_ref=src, dst_ref=dst, send_sem=s, recv_sem=r, device_id=to, device_id_type=MESH
        )
        copy.start()
        return copy

    pl.semaphore_wait(barrier, len(peers))

    f_col = [send(obj.at[p], right.at[p], fc_s.at[p], fc_r.at[p], lft) for p in range(4)]
    f_row = [send(obj.at[p], below.at[p], fr_s.at[p], fr_r.at[p], up) for p in range(4)]
    f_diag = [None] * 4

    def pass_on(p):
        f_col[p].wait_recv()
        f_diag[p] = send(right.at[p], diag.at[p], fd_s.at[p], fd_r.at[p], up)

    rows_of = lax.broadcasted_iota(jnp.int32, (W, W), 0)
    cols_of = lax.broadcasted_iota(jnp.int32, (W, W), 1)
    corners = [(offs[s, 0], offs[s, 1]) for s in range(CAP)]
    in_own_row = [rows_of >= r for r, _ in corners]
    in_own_col = [cols_of >= c for _, c in corners]

    for load in loads:
        load.wait()
    waves = [
        tuple(pltpu.roll(pltpu.roll(probe[j], r, 0), c, 1) for j in range(2)) for r, c in corners
    ]

    def window(p, s):
        top = jnp.where(in_own_col[s], own[p], right[p])
        low = jnp.where(in_own_col[s], below[p], diag[p])
        return jnp.where(in_own_row[s], top, low)

    def arrive(p):
        f_row[p].wait_recv()
        f_diag[p].wait_recv()

    pass_on(0)
    pass_on(1)
    arrive(0)
    arrive(1)
    patch1 = [(window(0, s), window(1, s)) for s in range(CAP)]
    moved = _two_sided([_mul(waves[s], patch1[s]) for s in range(CAP)], tab.at[0], False)
    pass_on(2)
    pass_on(3)
    arrive(2)
    arrive(3)
    patch2 = [(window(2, s), window(3, s)) for s in range(CAP)]
    far = _two_sided([_mul(moved[s], patch2[s]) for s in range(CAP)], tab.at[1], False)
    live_count = cnt[0]
    back = []
    for s in range(CAP):
        re, im = far[s]
        live = jnp.where(live_count > s, 2.0, 0.0).astype(F32)
        excess = (re * re + im * im - meas[s]) * live
        back.append((re * excess, im * excess))
    back = _two_sided(back, tab.at[1], True)

    def spread(p, grads):
        parts = [jnp.zeros((W, W), F32)] * 4
        for s in range(CAP):
            top = jnp.where(in_own_row[s], grads[s], 0.0)
            low = jnp.where(in_own_row[s], 0.0, grads[s])
            parts[0] += jnp.where(in_own_col[s], top, 0.0)
            parts[1] += jnp.where(in_own_col[s], 0.0, top)
            parts[2] += jnp.where(in_own_col[s], low, 0.0)
            parts[3] += jnp.where(in_own_col[s], 0.0, low)
        g_own[p], g_right[p], g_below[p], g_diag[p] = parts

    b_below, b_diag, b_col = [None] * 4, [None] * 4, [None] * 4

    def send_down(p):
        b_diag[p] = send(g_diag.at[p], r_diag.at[p], bd_s.at[p], bd_r.at[p], down)
        b_below[p] = send(g_below.at[p], r_below.at[p], bb_s.at[p], bb_r.at[p], down)

    def send_right(p):
        b_diag[p].wait_recv()
        g_right[p] += r_diag[p]
        b_col[p] = send(g_right.at[p], r_right.at[p], bc_s.at[p], bc_r.at[p], rgt)

    grads = [_mul_conj(back[s], moved[s]) for s in range(CAP)]
    for j in range(2):
        spread(2 + j, [g[j] for g in grads])
        send_down(2 + j)
    back = _two_sided([_mul_conj(back[s], patch2[s]) for s in range(CAP)], tab.at[0], True)
    send_right(2)
    send_right(3)
    grads = [_mul_conj(back[s], waves[s]) for s in range(CAP)]
    for j in range(2):
        spread(j, [g[j] for g in grads])
        send_down(j)
    probe_grads = [_mul_conj(back[s], patch1[s]) for s in range(CAP)]
    for j in range(2):
        total = jnp.zeros((W, W), F32)
        for s, (r, c) in enumerate(corners):
            total += pltpu.roll(pltpu.roll(probe_grads[s][j], lax.rem(W - r, W), 0), lax.rem(W - c, W), 1)
        gp[j] = total

    to_core = send(gp.at[1 - core], core_in, core_s, core_r, partner)
    send_right(0)
    send_right(1)
    to_core.wait_recv()
    gp[core] += core_in[...]
    piece = x * 4 + y
    to_xy = []
    for k in range(1, 16):
        px, py = xy_peers[k]
        start = pl.multiple_of((px * 4 + py) * 8, 8)
        to_xy.append(
            send(gp.at[core, pl.ds(start, 8)], xy_in.at[k], xy_s.at[k], xy_r.at[k], at(px, py, z_lo, z_hi, core))
        )
    mine = pl.multiple_of(piece * 8, 8)
    total = gp[core, pl.ds(mine, 8)]
    for k in range(1, 16):
        to_xy[k - 1].wait_recv()
        total += xy_in[k]
    za_in[0] = total
    to_za = [send(za_in.at[0], za_in.at[k], za_s.at[k], za_r.at[k], za_peers[k]) for k in range(1, 4)]
    for copy in to_za:
        copy.wait_recv()
    zb_in[0] = (za_in[0] + za_in[1]) + (za_in[2] + za_in[3])
    to_zb = [send(zb_in.at[0], zb_in.at[k], zb_s.at[k], zb_r.at[k], zb_peers[k]) for k in range(1, 4)]
    for copy in to_zb:
        copy.wait_recv()
    total = (zb_in[0] + zb_in[1]) + (zb_in[2] + zb_in[3])
    plane[core, pl.ds(mine, 8)] = total * (1.0 / math.sqrt(n_row * n_col * CAP))
    to_ag = []
    for k in range(1, 16):
        px, py = xy_peers[k]
        to_ag.append(
            send(
                plane.at[core, pl.ds(mine, 8)], plane.at[core, pl.ds(mine, 8)], ag_s.at[k], ag_r.at[k],
                at(px, py, z_lo, z_hi, core),
            )
        )
    for copy in to_ag:
        copy.wait_recv()
    to_cg = send(plane.at[core], plane.at[core], cg_s, cg_r, partner)

    for p in (2, 3, 0, 1):
        b_below[p].wait_recv()
        g_own[p] += r_below[p]
    for p in (2, 3, 0, 1):
        b_col[p].wait_recv()
        out[p] = g_own[p] + r_right[p]
    to_cg.wait_recv()
    pout[...] = plane[...]
    for copy in f_col + f_row + f_diag + b_below + b_diag + b_col + to_xy + to_za + to_zb + to_ag + [to_core, to_cg]:
        copy.wait_send()


def _per_device(n_row, n_col, object_slices, probe_field, measured, offsets, counts):
    obj = object_slices.reshape(4, W, W)
    dma = pltpu.SemaphoreType.DMA
    tile = pltpu.VMEM((4, W, W), F32)
    any_, vmem, smem = (pl.BlockSpec(memory_space=m) for m in (pl.ANY, pltpu.VMEM, pltpu.SMEM))
    out, pout = pl.pallas_call(
        functools.partial(_kernel, n_row, n_col),
        out_shape=(jax.ShapeDtypeStruct((4, W, W), F32), jax.ShapeDtypeStruct((2, W, W), F32)),
        in_specs=[smem, smem, any_, any_, any_, any_],
        out_specs=(vmem, vmem),
        scratch_shapes=[tile] * 11
        + [
            pltpu.VMEM((2, W, W), F32),
            pltpu.VMEM((CAP, W, W), F32),
            pltpu.VMEM((2, 6, W, W), BF16),
            pltpu.VMEM((2, W, W), F32),
            pltpu.VMEM((W, W), F32),
            pltpu.VMEM((16, 8, W), F32),
            pltpu.VMEM((4, 8, W), F32),
            pltpu.VMEM((4, 8, W), F32),
            pltpu.VMEM((2, W, W), F32),
        ]
        + [dma((4,))] * 13
        + [dma, dma]
        + [dma((16,))] * 2
        + [dma((4,))] * 4
        + [dma((16,))] * 2
        + [dma, dma],
        compiler_params=pltpu.CompilerParams(
            collective_id=0, has_side_effects=True, vmem_limit_bytes=40 * 1024 * 1024
        ),
    )(offsets, counts, obj, probe_field, measured, jnp.asarray(_tables()))
    return out.reshape(object_slices.shape), pout


def solution(mesh):
    in_specs = (
        P(None, None, "row", "col"),
        P(),
        P(("row", "col"), None, None),
        P(("row", "col"), None),
        P(("row", "col")),
    )
    out_specs = (P(None, None, "row", "col"), P())
    return jax.shard_map(
        functools.partial(_per_device, mesh.shape["row"], mesh.shape["col"]),
        mesh=mesh,
        in_specs=in_specs,
        out_specs=out_specs,
        check_vma=False,
    )
```

time: 634 us -> 119 us (0.19)
  waiting for transfers between devices: 442 us -> 0 us
  Pallas kernels: 0 us -> 111 us
  starting transfers between devices: 89.4 us -> 0 us
  matrix products: 31.5 us -> 0 us
  local copies, waits for them, and re-layouts: 31.1 us -> 5.92 us
  other arithmetic: 25 us -> 0 us
  between operations: 15.3 us -> 1.3 us
    psum x1 -> x0, waiting for transfers between devices: 412 us -> none  [per_device(): summed = lax.psum(grad_probe, ('row', 'col'))]
    pallas_call x0 -> x1, Pallas kernels: none -> 111 us  [_per_device(): pl.pallas_call(functools.partial(_kernel, n_row, n_col), out_shape=(jax.S...]
    ppermute x4 -> x0, starting transfers between devices: 89.4 us -> none  [from_behind(): return lax.ppermute(x, axis, [(i, (i + by) % peers) for i in range(peers)])]
    dot_general x48 -> x0, matrix products: 31.5 us -> none  [matmul_high(): return jnp.matmul(left, right, precision=lax.Precision.HIGHEST)]
    ppermute x4 -> x0, waiting for transfers between devices: 29.3 us -> none  [from_behind(): return lax.ppermute(x, axis, [(i, (i + by) % peers) for i in range(peers)])]
    scatter-add x8 -> x0, other arithmetic: 21.4 us -> none
    scatter-add x12 -> x0, local copies, waits for them, and re-layouts: 20.6 us -> none
    gather x12 -> x0, local copies, waits for them, and re-layouts: 8.23 us -> none
  transfers between devices with their start and end apart: 5 -> 0, of which waited for: 3 -> 0; matrix products, arithmetic and copies ran while one was open for 1% -> 0% of each run, Pallas kernels for 0% -> 0%
where the time goes in v1:
time: 119 us
  Pallas kernels  111 us (93%)
  local copies, waits for them, and re-layouts  5.92 us (5%)
  between operations  1.3 us (1%)
    pallas_call x1, Pallas kernels, _per_device(): pl.pallas_call(functools.partial(_kernel, n_row, n_col), out_shape=(jax.S...  111 us
    unnamed x13, local copies, waits for them, and re-layouts  5.92 us

profile of v1, /device:TPU:1, one launch (start us, length us, event | category | flops | bytes accessed | tf_op | source)
XLA Modules:
  0.0 118.7 jit_solution(3642405052250890630)
XLA Ops:
  1.3 0.0 copy-start.4
  1.3 0.7 copy-done.4
  2.0 0.1 copy.8.offs
  2.0 0.0 copy-start
  2.1 1.0 copy-done
  3.0 0.0 copy-start.1
  3.0 0.9 copy-done.1
  4.0 0.0 copy-start.2
  4.0 0.9 copy-done.2
  4.9 0.0 copy-start.3
  4.9 0.9 copy-done.3
  5.9 111.5 %shard_map.77 = (f32[4,128,128]{2,1,0:T(8,128)S(1)}, f32[2,128,128]{2,1,0:T(8,128)S(1)}) custom-call(s32[4,2]{1,0:T(4,128)S(1)} %copy.8.offs, s32[1]{0:T(128)S(6)} %copy.11.cnt, f32[4,128,128]{2,1,0:T(8,128)S(1)} %bitcast.3, f32[2,128,128]{2,1,0:T(8,128)S(1)} %copy-done.3, f32[4,128,128]{2,1,0:T(8,128)S(1)} %copy-done.2, bf16[2,6,128,128]{3,2,1,0:T(8,128)(2,1)S(1)} %copy-done), custom_call_target="tpu_custom_call" | custom-call | tf_op jit(solution)/shard_map/pallas_call | solution.py:291
  117.3 0.7 copy.12
  118.0 0.7 copy.13
Async XLA Ops:
  1.3 0.7 copy-start.4
  2.0 1.0 copy-start
  3.0 0.9 copy-start.1
  4.0 0.9 copy-start.2
  4.9 0.9 copy-start.3

commit v2 on v1

--- a/solution.py
+++ b/solution.py
@@ -13,6 +13,9 @@
 PROP = 40.0
 W = 128
 CAP = 4
+SPLIT = 2
+PARTS = 4 * SPLIT
+AHEAD = 8
 MESH = pl.DeviceIdType.MESH
 F32 = jnp.float32
 BF16 = jnp.bfloat16
@@ -89,9 +92,9 @@
 def _kernel(
     n_row, n_col, offs, cnt, obj, probe_hbm, meas_hbm, tab_hbm, out, pout,
     own, right, below, diag, g_own, g_right, g_below, g_diag, r_right, r_below, r_diag,
-    probe, meas, tab, gp, core_in, xy_in, za_in, zb_in, plane,
+    probe, meas, tab, gp, core_in, xy_in, z_in, plane,
     local, fc_s, fc_r, fr_s, fr_r, fd_s, fd_r, bb_s, bb_r, bd_s, bd_r, bc_s, bc_r,
-    core_s, core_r, xy_s, xy_r, za_s, za_r, zb_s, zb_r, ag_s, ag_r, cg_s, cg_r,
+    core_s, core_r, xy_s, xy_r, z_s, z_r, ag_s, ag_r, cg_s, cg_r,
 ):
     row, col = lax.axis_index("row"), lax.axis_index("col")
     core = lax.rem(row, 2)
@@ -99,25 +102,25 @@
     x = row // 16
     z_hi = lax.rem(col, 2)
     y = col // 2
+    first, last = lax.rem(row, 16) == 0, lax.rem(row, 16) == 15
 
     def at(x_, y_, zl, zh, core_):
         return ((x_ * 8 + zl) * 2 + core_, y_ * 2 + zh)
 
-    up = (lax.rem(row + n_row - 1, n_row), col)
-    down = (lax.rem(row + 1, n_row), col)
-    lft = (row, lax.rem(col + n_col - 1, n_col))
-    rgt = (row, lax.rem(col + 1, n_col))
+    row_up, row_down = lax.rem(row + n_row - 1, n_row), lax.rem(row + 1, n_row)
+    col_left, col_right = lax.rem(col + n_col - 1, n_col), lax.rem(col + 1, n_col)
+    up, down, lft, rgt = (row_up, col), (row_down, col), (row, col_left), (row, col_right)
+    up_left, down_right = (row_up, col_left), (row_down, col_right)
     partner = at(x, y, z_lo, z_hi, 1 - core)
-    xy_peers = [
-        (_xor(x, k // 4), _xor(y, k % 4)) for k in range(16)
-    ]
-    za_peers = [at(x, y, (z_lo // 4) * 4 + _xor(lax.rem(z_lo, 4), k), z_hi, core) for k in range(4)]
-    zb_peers = [
-        at(x, y, lax.rem(z_lo + 4 * (k % 2), 8), z_hi if k < 2 else 1 - z_hi, core) for k in range(4)
-    ]
-    peers = [up, down, lft, rgt, partner]
+    xy_peers = [(_xor(x, k // 4), _xor(y, k % 4)) for k in range(16)]
+    z = z_hi * 8 + z_lo
+    z_peers = []
+    for k in range(16):
+        other = lax.rem(z + k, 16)
+        z_peers.append(at(x, y, lax.rem(other, 8), other // 8, core))
+    peers = [up, down, lft, rgt, partner, up_left, down_right]
     peers += [at(px, py, z_lo, z_hi, core) for px, py in xy_peers[1:]]
-    peers += za_peers[1:] + zb_peers[1:]
+    peers += z_peers[1:]
     barrier = pltpu.get_barrier_semaphore()
     for peer in peers:
         pl.semaphore_signal(barrier, inc=1, device_id=peer, device_id_type=MESH)
@@ -131,26 +134,47 @@
     for load in loads:
         load.start()
 
-    def send(src, dst, s, r, to):
-        copy = pltpu.make_async_remote_copy(
+    def remote(src, dst, s, r, to):
+        return pltpu.make_async_remote_copy(
             src_ref=src, dst_ref=dst, send_sem=s, recv_sem=r, device_id=to, device_id_type=MESH
         )
+
+    def send(src, dst, s, r, to):
+        copy = remote(src, dst, s, r, to)
         copy.start()
         return copy
 
     pl.semaphore_wait(barrier, len(peers))
 
-    f_col = [send(obj.at[p], right.at[p], fc_s.at[p], fc_r.at[p], lft) for p in range(4)]
+    def part(ref, i):
+        return ref.at[i // SPLIT, pl.ds((i % SPLIT) * (W // SPLIT), W // SPLIT)]
+
+    def send_left(i):
+        return send(part(obj, i), part(right, i), fc_s.at[i], fc_r.at[i], lft)
+
+    f_col = [send_left(i) for i in range(AHEAD)]
     f_row = [send(obj.at[p], below.at[p], fr_s.at[p], fr_r.at[p], up) for p in range(4)]
-    f_diag = [None] * 4
-
-    def pass_on(p):
-        f_col[p].wait_recv()
-        f_diag[p] = send(right.at[p], diag.at[p], fd_s.at[p], fd_r.at[p], up)
+    f_diag = [remote(part(right, i), part(diag, i), fd_s.at[i], fd_r.at[i], up) for i in range(PARTS)]
+
+    @pl.when(first)
+    def _():
+        for i in range(PARTS):
+            send(part(obj, i), part(diag, i), fd_s.at[i], fd_r.at[i], up_left)
+
+    def pass_on(i):
+        f_col[i].wait_recv()
+
+        @pl.when(jnp.logical_not(first))
+        def _():
+            f_diag[i].start()
+
+        if i + AHEAD < PARTS:
+            f_col[i].wait_send()
+            f_col.append(send_left(i + AHEAD))
 
     rows_of = lax.broadcasted_iota(jnp.int32, (W, W), 0)
     cols_of = lax.broadcasted_iota(jnp.int32, (W, W), 1)
-    corners = [(offs[s, 0], offs[s, 1]) for s in range(CAP)]
+    corners = [(offs[0, s], offs[1, s]) for s in range(CAP)]
     in_own_row = [rows_of >= r for r, _ in corners]
     in_own_col = [cols_of >= c for _, c in corners]
 
@@ -167,16 +191,18 @@
 
     def arrive(p):
         f_row[p].wait_recv()
-        f_diag[p].wait_recv()
-
-    pass_on(0)
-    pass_on(1)
+        for i in range(p * SPLIT, (p + 1) * SPLIT):
+            f_diag[i].wait_recv()
+
+    early = 2 * SPLIT + 1
+    for i in range(early):
+        pass_on(i)
     arrive(0)
     arrive(1)
     patch1 = [(window(0, s), window(1, s)) for s in range(CAP)]
     moved = _two_sided([_mul(waves[s], patch1[s]) for s in range(CAP)], tab.at[0], False)
-    pass_on(2)
-    pass_on(3)
+    for i in range(early, PARTS):
+        pass_on(i)
     arrive(2)
     arrive(3)
     patch2 = [(window(2, s), window(3, s)) for s in range(CAP)]
@@ -201,28 +227,40 @@
             parts[3] += jnp.where(in_own_col[s], 0.0, low)
         g_own[p], g_right[p], g_below[p], g_diag[p] = parts
 
-    b_below, b_diag, b_col = [None] * 4, [None] * 4, [None] * 4
-
-    def send_down(p):
-        b_diag[p] = send(g_diag.at[p], r_diag.at[p], bd_s.at[p], bd_r.at[p], down)
+    b_diag = [remote(g_diag.at[p], r_diag.at[p], bd_s.at[p], bd_r.at[p], down) for p in range(4)]
+    b_below, b_col = [None] * 4, [None] * 4
+
+    def send_diag(p):
+        @pl.when(jnp.logical_not(last))
+        def _():
+            b_diag[p].start()
+
+        @pl.when(last)
+        def _():
+            send(g_diag.at[p], r_diag.at[p], bd_s.at[p], bd_r.at[p], down_right)
+
+    def send_below(p):
         b_below[p] = send(g_below.at[p], r_below.at[p], bb_s.at[p], bb_r.at[p], down)
 
     def send_right(p):
-        b_diag[p].wait_recv()
-        g_right[p] += r_diag[p]
+        @pl.when(jnp.logical_not(first))
+        def _():
+            b_diag[p].wait_recv()
+            g_right[p] += r_diag[p]
+
         b_col[p] = send(g_right.at[p], r_right.at[p], bc_s.at[p], bc_r.at[p], rgt)
 
     grads = [_mul_conj(back[s], moved[s]) for s in range(CAP)]
     for j in range(2):
         spread(2 + j, [g[j] for g in grads])
-        send_down(2 + j)
+        send_diag(2 + j)
     back = _two_sided([_mul_conj(back[s], patch2[s]) for s in range(CAP)], tab.at[0], True)
-    send_right(2)
-    send_right(3)
     grads = [_mul_conj(back[s], waves[s]) for s in range(CAP)]
     for j in range(2):
         spread(j, [g[j] for g in grads])
-        send_down(j)
+        send_diag(j)
+    send_right(2)
+    send_right(3)
     probe_grads = [_mul_conj(back[s], patch1[s]) for s in range(CAP)]
     for j in range(2):
         total = jnp.zeros((W, W), F32)
@@ -230,43 +268,39 @@
             total += pltpu.roll(pltpu.roll(probe_grads[s][j], lax.rem(W - r, W), 0), lax.rem(W - c, W), 1)
         gp[j] = total
 
+    for p in (2, 3, 0, 1):
+        send_below(p)
     to_core = send(gp.at[1 - core], core_in, core_s, core_r, partner)
-    send_right(0)
-    send_right(1)
     to_core.wait_recv()
     gp[core] += core_in[...]
-    piece = x * 4 + y
+    mine = pl.multiple_of((x * 4 + y) * 8, 8)
     to_xy = []
-    for k in range(1, 16):
+    for k in (1, 2, 3, 4, 5, 6, 7, 8, 9, 10, 11, 12, 13, 14, 15):
         px, py = xy_peers[k]
         start = pl.multiple_of((px * 4 + py) * 8, 8)
-        to_xy.append(
-            send(gp.at[core, pl.ds(start, 8)], xy_in.at[k], xy_s.at[k], xy_r.at[k], at(px, py, z_lo, z_hi, core))
-        )
-    mine = pl.multiple_of(piece * 8, 8)
+        to_xy.append(send(gp.at[core, pl.ds(start, 8)], xy_in.at[k], xy_s.at[k], xy_r.at[k], at(px, py, z_lo, z_hi, core)))
     total = gp[core, pl.ds(mine, 8)]
     for k in range(1, 16):
         to_xy[k - 1].wait_recv()
+    for k in range(1, 16):
         total += xy_in[k]
-    za_in[0] = total
-    to_za = [send(za_in.at[0], za_in.at[k], za_s.at[k], za_r.at[k], za_peers[k]) for k in range(1, 4)]
-    for copy in to_za:
-        copy.wait_recv()
-    zb_in[0] = (za_in[0] + za_in[1]) + (za_in[2] + za_in[3])
-    to_zb = [send(zb_in.at[0], zb_in.at[k], zb_s.at[k], zb_r.at[k], zb_peers[k]) for k in range(1, 4)]
-    for copy in to_zb:
-        copy.wait_recv()
-    total = (zb_in[0] + zb_in[1]) + (zb_in[2] + zb_in[3])
+    z_in[z] = total
+    to_z = []
+    for k in (1, 2, 3, 4, 5, 6, 7, 8, 9, 10, 11, 12, 13, 14, 15):
+        to_z.append(send(z_in.at[z], z_in.at[z], z_s.at[k], z_r.at[z], z_peers[k]))
+    for k in range(1, 16):
+        remote(z_in.at[z], z_in.at[z], z_s.at[k], z_r.at[lax.rem(z + k, 16)], z_peers[k]).wait_recv()
+    total = z_in[0]
+    for k in range(1, 16):
+        total += z_in[k]
     plane[core, pl.ds(mine, 8)] = total * (1.0 / math.sqrt(n_row * n_col * CAP))
+    send_right(0)
+    send_right(1)
     to_ag = []
-    for k in range(1, 16):
+    for k in (1, 2, 3, 4, 5, 6, 7, 8, 9, 10, 11, 12, 13, 14, 15):
         px, py = xy_peers[k]
-        to_ag.append(
-            send(
-                plane.at[core, pl.ds(mine, 8)], plane.at[core, pl.ds(mine, 8)], ag_s.at[k], ag_r.at[k],
-                at(px, py, z_lo, z_hi, core),
-            )
-        )
+        held = plane.at[core, pl.ds(mine, 8)]
+        to_ag.append(send(held, held, ag_s.at[k], ag_r.at[k], at(px, py, z_lo, z_hi, core)))
     for copy in to_ag:
         copy.wait_recv()
     to_cg = send(plane.at[core], plane.at[core], cg_s, cg_r, partner)
@@ -274,12 +308,19 @@
     for p in (2, 3, 0, 1):
         b_below[p].wait_recv()
         g_own[p] += r_below[p]
+
+        @pl.when(first)
+        def _():
+            b_diag[p].wait_recv()
+            g_own[p] += r_diag[p]
+
     for p in (2, 3, 0, 1):
         b_col[p].wait_recv()
         out[p] = g_own[p] + r_right[p]
     to_cg.wait_recv()
     pout[...] = plane[...]
-    for copy in f_col + f_row + f_diag + b_below + b_diag + b_col + to_xy + to_za + to_zb + to_ag + [to_core, to_cg]:
+    sent = f_col[PARTS - AHEAD :] + f_row + f_diag + b_below + b_diag + b_col
+    for copy in sent + to_xy + to_z + to_ag + [to_core, to_cg]:
         copy.wait_send()
 
 
@@ -301,20 +342,21 @@
             pltpu.VMEM((2, W, W), F32),
             pltpu.VMEM((W, W), F32),
             pltpu.VMEM((16, 8, W), F32),
-            pltpu.VMEM((4, 8, W), F32),
-            pltpu.VMEM((4, 8, W), F32),
+            pltpu.VMEM((16, 8, W), F32),
             pltpu.VMEM((2, W, W), F32),
         ]
-        + [dma((4,))] * 13
+        + [dma((4,))]
+        + [dma((PARTS,))] * 2
+        + [dma((4,))] * 2
+        + [dma((PARTS,))] * 2
+        + [dma((4,))] * 6
         + [dma, dma]
-        + [dma((16,))] * 2
-        + [dma((4,))] * 4
-        + [dma((16,))] * 2
+        + [dma((16,))] * 6
         + [dma, dma],
         compiler_params=pltpu.CompilerParams(
-            collective_id=0, has_side_effects=True, vmem_limit_bytes=40 * 1024 * 1024
+            collective_id=0, has_side_effects=True, vmem_limit_bytes=60 * 1024 * 1024
         ),
-    )(offsets, counts, obj, probe_field, measured, jnp.asarray(_tables()))
+    )(offsets.T, counts, obj, probe_field, measured, jnp.asarray(_tables()))
     return out.reshape(object_slices.shape), pout
 
 

time: 119 us -> 98 us (0.82)
  the two profiles are of different devices: /device:TPU:1 before, /device:TPU:34 now
where the time goes in v2:
time: 98 us; the launch traced here: 97.9 us
  Pallas kernels  94.2 us (96%)
  local copies, waits for them, and re-layouts  2.36 us (2%)
  between operations  1.29 us (1%)
    pallas_call x1, Pallas kernels, _per_device(): pl.pallas_call(functools.partial(_kernel, n_row, n_col), out_shape=(jax.S...  94.2 us
    unnamed x4, local copies, waits for them, and re-layouts  2.36 us

profile of v2, /device:TPU:34, one launch (start us, length us, event | category | flops | bytes accessed | tf_op | source)
XLA Modules:
  0.0 97.9 jit_solution(6315279683581214505)
XLA Ops:
  1.3 94.2 %shard_map.77 = (f32[4,128,128]{2,1,0:T(8,128)}, f32[2,128,128]{2,1,0:T(8,128)}) custom-call(s32[2,4]{1,0:T(2,128)} %bitcast.5, s32[1]{0:T(128)S(6)} %copy.10.cnt, f32[4,128,128]{2,1,0:T(8,128)} %bitcast.3, f32[2,128,128]{2,1,0:T(8,128)} %probe_hbm.1, f32[4,128,128]{2,1,0:T(8,128)} %meas_hbm.1, bf16[2,6,128,128]{3,2,1,0:T(8,128)(2,1)} %constant.2.clone.tab_hbm), custom_call_target="tpu_custom_call" | custom-call | tf_op jit(solution)/shard_map/pallas_call | solution.py:332
  95.5 0.0 copy-start
  95.5 1.7 %copy.11 = f32[2,2,128,128]{3,2,1,0:T(8,128)} copy(f32[2,2,128,128]{3,2,1,0:T(8,128)} %bitcast.4) | data formatting | bytes 524288
  97.2 0.0 copy-done
  97.2 0.7 copy.12
Async XLA Ops:
  95.5 1.7 %copy-start = (f32[2,128,128]{2,1,0:T(8,128)S(1)}, f32[2,128,128]{2,1,0:T(8,128)}, u32[]{:S(2)}) copy-start(f32[2,128,128]{2,1,0:T(8,128)} %get-tuple-element.9) | copy-start | bytes 393220

commit v3 on v2

--- a/solution.py
+++ b/solution.py
@@ -113,14 +113,11 @@
     up_left, down_right = (row_up, col_left), (row_down, col_right)
     partner = at(x, y, z_lo, z_hi, 1 - core)
     xy_peers = [(_xor(x, k // 4), _xor(y, k % 4)) for k in range(16)]
-    z = z_hi * 8 + z_lo
-    z_peers = []
-    for k in range(16):
-        other = lax.rem(z + k, 16)
-        z_peers.append(at(x, y, lax.rem(other, 8), other // 8, core))
+    za_peers = [at(x, y, (z_lo // 4) * 4 + _xor(lax.rem(z_lo, 4), k), z_hi, core) for k in range(4)]
+    zb_peers = [at(x, y, lax.rem(z_lo + 4 * (k % 2), 8), z_hi if k < 2 else 1 - z_hi, core) for k in range(4)]
     peers = [up, down, lft, rgt, partner, up_left, down_right]
     peers += [at(px, py, z_lo, z_hi, core) for px, py in xy_peers[1:]]
-    peers += z_peers[1:]
+    peers += za_peers[1:] + zb_peers[1:]
     barrier = pltpu.get_barrier_semaphore()
     for peer in peers:
         pl.semaphore_signal(barrier, inc=1, device_id=peer, device_id_type=MESH)
@@ -259,8 +256,6 @@
     for j in range(2):
         spread(j, [g[j] for g in grads])
         send_diag(j)
-    send_right(2)
-    send_right(3)
     probe_grads = [_mul_conj(back[s], patch1[s]) for s in range(CAP)]
     for j in range(2):
         total = jnp.zeros((W, W), F32)
@@ -268,8 +263,6 @@
             total += pltpu.roll(pltpu.roll(probe_grads[s][j], lax.rem(W - r, W), 0), lax.rem(W - c, W), 1)
         gp[j] = total
 
-    for p in (2, 3, 0, 1):
-        send_below(p)
     to_core = send(gp.at[1 - core], core_in, core_s, core_r, partner)
     to_core.wait_recv()
     gp[core] += core_in[...]
@@ -279,20 +272,24 @@
         px, py = xy_peers[k]
         start = pl.multiple_of((px * 4 + py) * 8, 8)
         to_xy.append(send(gp.at[core, pl.ds(start, 8)], xy_in.at[k], xy_s.at[k], xy_r.at[k], at(px, py, z_lo, z_hi, core)))
+    send_right(2)
     total = gp[core, pl.ds(mine, 8)]
     for k in range(1, 16):
         to_xy[k - 1].wait_recv()
     for k in range(1, 16):
         total += xy_in[k]
-    z_in[z] = total
-    to_z = []
-    for k in (1, 2, 3, 4, 5, 6, 7, 8, 9, 10, 11, 12, 13, 14, 15):
-        to_z.append(send(z_in.at[z], z_in.at[z], z_s.at[k], z_r.at[z], z_peers[k]))
-    for k in range(1, 16):
-        remote(z_in.at[z], z_in.at[z], z_s.at[k], z_r.at[lax.rem(z + k, 16)], z_peers[k]).wait_recv()
-    total = z_in[0]
-    for k in range(1, 16):
-        total += z_in[k]
+    z_in[0] = total
+    to_z = [send(z_in.at[0], z_in.at[k], z_s.at[k], z_r.at[k], za_peers[k]) for k in range(1, 4)]
+    send_right(3)
+    for copy in to_z[:3]:
+        copy.wait_recv()
+    z_in[4] = (z_in[0] + z_in[1]) + (z_in[2] + z_in[3])
+    to_z += [send(z_in.at[4], z_in.at[4 + k], z_s.at[4 + k], z_r.at[4 + k], zb_peers[k]) for k in range(1, 4)]
+    for p in (2, 3, 0, 1):
+        send_below(p)
+    for copy in to_z[3:]:
+        copy.wait_recv()
+    total = (z_in[4] + z_in[5]) + (z_in[6] + z_in[7])
     plane[core, pl.ds(mine, 8)] = total * (1.0 / math.sqrt(n_row * n_col * CAP))
     send_right(0)
     send_right(1)
@@ -342,7 +339,7 @@
             pltpu.VMEM((2, W, W), F32),
             pltpu.VMEM((W, W), F32),
             pltpu.VMEM((16, 8, W), F32),
-            pltpu.VMEM((16, 8, W), F32),
+            pltpu.VMEM((8, 8, W), F32),
             pltpu.VMEM((2, W, W), F32),
         ]
         + [dma((4,))]
@@ -351,7 +348,9 @@
         + [dma((PARTS,))] * 2
         + [dma((4,))] * 6
         + [dma, dma]
-        + [dma((16,))] * 6
+        + [dma((16,))] * 2
+        + [dma((8,))] * 2
+        + [dma((16,))] * 2
         + [dma, dma],
         compiler_params=pltpu.CompilerParams(
             collective_id=0, has_side_effects=True, vmem_limit_bytes=60 * 1024 * 1024

time: 98 us -> 96.8 us (0.988)
  the two profiles are of different devices: /device:TPU:34 before, /device:TPU:36 now
where the time goes in v3:
time: 96.8 us; the launch traced here: 96.6 us
  Pallas kernels  93 us (96%)
  local copies, waits for them, and re-layouts  2.36 us (2%)
  between operations  1.29 us (1%)
    pallas_call x1, Pallas kernels, _per_device(): pl.pallas_call(functools.partial(_kernel, n_row, n_col), out_shape=(jax.S...  93 us
    unnamed x4, local copies, waits for them, and re-layouts  2.36 us

profile of v3, /device:TPU:36, one launch (start us, length us, event | category | flops | bytes accessed | tf_op | source)
XLA Modules:
  0.0 96.6 jit_solution(296173607881958063)
XLA Ops:
  1.3 93.0 %shard_map.77 = (f32[4,128,128]{2,1,0:T(8,128)}, f32[2,128,128]{2,1,0:T(8,128)}) custom-call(s32[2,4]{1,0:T(2,128)} %bitcast.5, s32[1]{0:T(128)S(6)} %copy.10.cnt, f32[4,128,128]{2,1,0:T(8,128)} %bitcast.3, f32[2,128,128]{2,1,0:T(8,128)} %probe_hbm.1, f32[4,128,128]{2,1,0:T(8,128)} %meas_hbm.1, bf16[2,6,128,128]{3,2,1,0:T(8,128)(2,1)} %constant.2.clone.tab_hbm), custom_call_target="tpu_custom_call" | custom-call | tf_op jit(solution)/shard_map/pallas_call | solution.py:329
  94.3 0.0 copy-start
  94.3 1.7 %copy.11 = f32[2,2,128,128]{3,2,1,0:T(8,128)} copy(f32[2,2,128,128]{3,2,1,0:T(8,128)} %bitcast.4) | data formatting | bytes 524288
  96.0 0.0 copy-done
  96.0 0.7 copy.12
Async XLA Ops:
  94.3 1.7 %copy-start = (f32[2,128,128]{2,1,0:T(8,128)S(1)}, f32[2,128,128]{2,1,0:T(8,128)}, u32[]{:S(2)}) copy-start(f32[2,128,128]{2,1,0:T(8,128)} %get-tuple-element.9) | copy-start | bytes 393220

commit v4 on v3

--- a/solution.py
+++ b/solution.py
@@ -264,6 +264,7 @@
         gp[j] = total
 
     to_core = send(gp.at[1 - core], core_in, core_s, core_r, partner)
+    send_right(2)
     to_core.wait_recv()
     gp[core] += core_in[...]
     mine = pl.multiple_of((x * 4 + y) * 8, 8)
@@ -272,7 +273,6 @@
         px, py = xy_peers[k]
         start = pl.multiple_of((px * 4 + py) * 8, 8)
         to_xy.append(send(gp.at[core, pl.ds(start, 8)], xy_in.at[k], xy_s.at[k], xy_r.at[k], at(px, py, z_lo, z_hi, core)))
-    send_right(2)
     total = gp[core, pl.ds(mine, 8)]
     for k in range(1, 16):
         to_xy[k - 1].wait_recv()

time: 96.8 us -> 95.2 us (0.983)
  the two profiles are of different devices: /device:TPU:36 before, /device:TPU:96 now
where the time goes in v4:
time: 95.2 us; the launch traced here: 95 us
  Pallas kernels  91.4 us (96%)
  local copies, waits for them, and re-layouts  2.36 us (2%)
  between operations  1.29 us (1%)
    pallas_call x1, Pallas kernels, _per_device(): pl.pallas_call(functools.partial(_kernel, n_row, n_col), out_shape=(jax.S...  91.4 us
    unnamed x4, local copies, waits for them, and re-layouts  2.36 us

profile of v4, /device:TPU:96, one launch (start us, length us, event | category | flops | bytes accessed | tf_op | source)
XLA Modules:
  0.0 95.0 jit_solution(3754698343137486620)
XLA Ops:
  1.3 91.4 %shard_map.77 = (f32[4,128,128]{2,1,0:T(8,128)}, f32[2,128,128]{2,1,0:T(8,128)}) custom-call(s32[2,4]{1,0:T(2,128)} %bitcast.5, s32[1]{0:T(128)S(6)} %copy.10.cnt, f32[4,128,128]{2,1,0:T(8,128)} %bitcast.3, f32[2,128,128]{2,1,0:T(8,128)} %probe_hbm.1, f32[4,128,128]{2,1,0:T(8,128)} %meas_hbm.1, bf16[2,6,128,128]{3,2,1,0:T(8,128)(2,1)} %constant.2.clone.tab_hbm), custom_call_target="tpu_custom_call" | custom-call | tf_op jit(solution)/shard_map/pallas_call | solution.py:329
  92.7 0.0 copy-start
  92.7 1.7 %copy.11 = f32[2,2,128,128]{3,2,1,0:T(8,128)} copy(f32[2,2,128,128]{3,2,1,0:T(8,128)} %bitcast.4) | data formatting | bytes 524288
  94.4 0.0 copy-done
  94.4 0.7 copy.12
Async XLA Ops:
  92.7 1.7 %copy-start = (f32[2,128,128]{2,1,0:T(8,128)S(1)}, f32[2,128,128]{2,1,0:T(8,128)}, u32[]{:S(2)}) copy-start(f32[2,128,128]{2,1,0:T(8,128)} %get-tuple-element.9) | copy-start | bytes 393220

commit v5 on v4

--- a/solution.py
+++ b/solution.py
@@ -291,13 +291,13 @@
         copy.wait_recv()
     total = (z_in[4] + z_in[5]) + (z_in[6] + z_in[7])
     plane[core, pl.ds(mine, 8)] = total * (1.0 / math.sqrt(n_row * n_col * CAP))
-    send_right(0)
-    send_right(1)
     to_ag = []
     for k in (1, 2, 3, 4, 5, 6, 7, 8, 9, 10, 11, 12, 13, 14, 15):
         px, py = xy_peers[k]
         held = plane.at[core, pl.ds(mine, 8)]
         to_ag.append(send(held, held, ag_s.at[k], ag_r.at[k], at(px, py, z_lo, z_hi, core)))
+    send_right(0)
+    send_right(1)
     for copy in to_ag:
         copy.wait_recv()
     to_cg = send(plane.at[core], plane.at[core], cg_s, cg_r, partner)

time: 95.2 us -> 95.2 us (level)
  no operation moved by 1% of the time
where the time goes in v5:
time: 95.2 us; the launch traced here: 95.1 us
  Pallas kernels  91.4 us (96%)
  local copies, waits for them, and re-layouts  2.36 us (2%)
  between operations  1.29 us (1%)
    pallas_call x1, Pallas kernels, _per_device(): pl.pallas_call(functools.partial(_kernel, n_row, n_col), out_shape=(jax.S...  91.4 us
    unnamed x4, local copies, waits for them, and re-layouts  2.36 us

profile of v5, /device:TPU:96, one launch (start us, length us, event | category | flops | bytes accessed | tf_op | source)
XLA Modules:
  0.0 95.1 jit_solution(5241449646393461801)
XLA Ops:
  1.3 91.4 %shard_map.77 = (f32[4,128,128]{2,1,0:T(8,128)}, f32[2,128,128]{2,1,0:T(8,128)}) custom-call(s32[2,4]{1,0:T(2,128)} %bitcast.5, s32[1]{0:T(128)S(6)} %copy.10.cnt, f32[4,128,128]{2,1,0:T(8,128)} %bitcast.3, f32[2,128,128]{2,1,0:T(8,128)} %probe_hbm.1, f32[4,128,128]{2,1,0:T(8,128)} %meas_hbm.1, bf16[2,6,128,128]{3,2,1,0:T(8,128)(2,1)} %constant.2.clone.tab_hbm), custom_call_target="tpu_custom_call" | custom-call | tf_op jit(solution)/shard_map/pallas_call | solution.py:329
  92.7 0.0 copy-start
  92.7 1.7 %copy.11 = f32[2,2,128,128]{3,2,1,0:T(8,128)} copy(f32[2,2,128,128]{3,2,1,0:T(8,128)} %bitcast.4) | data formatting | bytes 524288
  94.4 0.0 copy-done
  94.4 0.7 copy.12
Async XLA Ops:
  92.7 1.7 %copy-start = (f32[2,128,128]{2,1,0:T(8,128)S(1)}, f32[2,128,128]{2,1,0:T(8,128)}, u32[]{:S(2)}) copy-start(f32[2,128,128]{2,1,0:T(8,128)} %get-tuple-element.9) | copy-start | bytes 393220
